TPU v7x, 32 devices: a whole 2x2x4 slice. The times are simulated.
32 devices in a mesh: dp: 4 (over x, core), seq: 8 (over z, y).
Axes of the slice: x: 2, y: 2, z: 4, core: 2. Of those that a mesh axis runs over, the one named last changes fastest.
Arguments:
- queries: bfloat16 [4, 2048, 2048], P('dp', 'seq'), may hold values from -8 to 8
- key_states: bfloat16 [4, 2048, 512], P('dp', 'seq'), may hold values from -6 to 6
- value_states: bfloat16 [4, 2048, 512], P('dp', 'seq'), may hold values from -6 to 6
- block_picks: int32 [4, 3, 8], P('dp'), may hold values from 0 to 1
- out_weight: bfloat16 [2048, 2048], P(('dp', 'seq')), may hold values from -0.5 to 0.5
- out_grad: bfloat16 [4, 2048, 2048], P('dp', 'seq'), may hold values from -4 to 4
Outputs:
- layer_out: bfloat16 [4, 2048, 2048], P('dp', 'seq')
- query_grad: bfloat16 [4, 2048, 2048], P('dp', 'seq')
- key_grad: bfloat16 [4, 2048, 512], P('dp', 'seq')
- value_grad: bfloat16 [4, 2048, 512], P('dp', 'seq')
All inputs are finite; a program needn't handle non-finite values.
Results may differ from a plain program's by a relative error of at most 0.025.
Values may be sent and summed in bfloat16 or wider, within the bound.
A program may use at most 128 MiB of HBM per device.

v0:
```python
import math
import jax
import jax.numpy as jnp
from jax import lax
from jax.sharding import PartitionSpec as P

HEAD_DIM = 128
BLOCK = 128
neg_fill = -1e30


def shifted(block, axis, distance):
    devices = range(lax.axis_size(axis))
    route = [(i - distance, i) for i in devices if i - distance in devices]
    return lax.ppermute(block, axis, route)


def shards(queries, key_states, value_states, block_picks, out_weight, out_grad):
    query_rows = queries[0]
    key_rows = key_states[0]
    value_rows = value_states[0]
    grad_rows = out_grad[0]
    picks_here = block_picks[0]
    tok_count = query_rows.shape[0]
    q_cols = query_rows.shape[1]
    kv_cols = key_rows.shape[1]
    kv_count = kv_cols // HEAD_DIM
    group_size = q_cols // kv_cols
    score_scale = 1.0 / math.sqrt(HEAD_DIM)
    seq_count = lax.axis_size("seq")
    level_count = seq_count.bit_length() - 1
    shard_index = lax.axis_index("seq")
    far_keys = []
    far_values = []
    for level_index in range(level_count):
        distance = 1 << level_index
        got_keys, got_values = shifted((key_rows, value_rows), "seq", distance)
        row_begin = picks_here[level_index, shard_index] * BLOCK
        far_keys.append(lax.dynamic_slice_in_dim(got_keys, row_begin, BLOCK, 0))
        far_values.append(lax.dynamic_slice_in_dim(got_values, row_begin, BLOCK, 0))
    all_keys = jnp.concatenate([key_rows] + far_keys, 0)
    all_values = jnp.concatenate([value_rows] + far_values, 0)
    key_total = all_keys.shape[0]
    row_ids = lax.broadcasted_iota(jnp.int32, (tok_count, key_total), 0)
    col_ids = lax.broadcasted_iota(jnp.int32, (tok_count, key_total), 1)
    far_level = jnp.maximum(col_ids - tok_count, 0) // BLOCK
    far_seen = shard_index >= jnp.left_shift(jnp.int32(1), far_level)
    visible = jnp.where(col_ids < tok_count, col_ids <= row_ids, far_seen)
    whole_weight = lax.all_gather(out_weight, ("dp", "seq"), axis=0, tiled=True)
    attn_grad = lax.dot_general(
        grad_rows, whole_weight, (((1,), (1,)), ((), ())), preferred_element_type=jnp.float32
    )
    attn_grad = attn_grad.astype(jnp.bfloat16)
    query_heads = query_rows.reshape(tok_count, kv_count, group_size, HEAD_DIM)
    key_heads = all_keys.reshape(key_total, kv_count, HEAD_DIM)
    value_heads = all_values.reshape(key_total, kv_count, HEAD_DIM)
    grad_heads = attn_grad.reshape(tok_count, kv_count, group_size, HEAD_DIM)
    attn_parts = []
    dq_parts = []
    dk_parts = []
    dv_parts = []
    for group_index in range(kv_count):
        query_group = query_heads[:, group_index]
        key_group = key_heads[:, group_index]
        value_group = value_heads[:, group_index]
        grad_group = grad_heads[:, group_index]
        scores = (
            jnp.einsum("tgd,sd->gts", query_group, key_group, preferred_element_type=jnp.float32)
            * score_scale
        )
        scores = jnp.where(visible[None], scores, neg_fill)
        row_max = jnp.max(scores, axis=-1, keepdims=True)
        exp_scores = jnp.exp(scores - row_max)
        probs = exp_scores / jnp.sum(exp_scores, axis=-1, keepdims=True)
        probs_low = probs.astype(jnp.bfloat16)
        attn_group = jnp.einsum(
            "gts,sd->tgd", probs_low, value_group, preferred_element_type=jnp.float32
        ).astype(jnp.bfloat16)
        row_delta = jnp.einsum(
            "tgd,tgd->gt", grad_group, attn_group, preferred_element_type=jnp.float32
        )[:, :, None]
        prob_grad = jnp.einsum(
            "tgd,sd->gts", grad_group, value_group, preferred_element_type=jnp.float32
        )
        score_low = (probs * (prob_grad - row_delta)).astype(jnp.bfloat16)
        dq_parts.append(
            (
                jnp.einsum("gts,sd->tgd", score_low, key_group, preferred_element_type=jnp.float32)
                * score_scale
            ).astype(jnp.bfloat16)
        )
        dk_parts.append(
            jnp.einsum("gts,tgd->sd", score_low, query_group, preferred_element_type=jnp.float32)
            * score_scale
        )
        dv_parts.append(
            jnp.einsum("gts,tgd->sd", probs_low, grad_group, preferred_element_type=jnp.float32)
        )
        attn_parts.append(attn_group)
    attn_all = jnp.stack(attn_parts, 1).reshape(tok_count, q_cols)
    query_grad = jnp.stack(dq_parts, 1).reshape(tok_count, q_cols)
    key_terms = jnp.stack(dk_parts, 1).reshape(key_total, kv_cols)
    value_terms = jnp.stack(dv_parts, 1).reshape(key_total, kv_cols)
    layer_sum = jnp.dot(attn_all, whole_weight, preferred_element_type=jnp.float32)
    layer_out = layer_sum.astype(jnp.bfloat16)
    key_grad = key_terms[:tok_count]
    value_grad = value_terms[:tok_count]
    for level_index in range(level_count):
        distance = 1 << level_index
        begin = tok_count + level_index * BLOCK
        back_keys, back_values = shifted(
            (key_terms[begin : begin + BLOCK], value_terms[begin : begin + BLOCK]), "seq", -distance
        )
        source = jnp.minimum(shard_index + distance, seq_count - 1)
        row_begin = picks_here[level_index, source] * BLOCK
        key_grad = lax.dynamic_update_slice_in_dim(
            key_grad,
            lax.dynamic_slice_in_dim(key_grad, row_begin, BLOCK, 0) + back_keys,
            row_begin,
            0,
        )
        value_grad = lax.dynamic_update_slice_in_dim(
            value_grad,
            lax.dynamic_slice_in_dim(value_grad, row_begin, BLOCK, 0) + back_values,
            row_begin,
            0,
        )
    return (
        layer_out[None],
        query_grad[None],
        key_grad.astype(jnp.bfloat16)[None],
        value_grad.astype(jnp.bfloat16)[None],
    )


def solution(mesh):
    return jax.shard_map(
        shards,
        mesh=mesh,
        in_specs=(
            P("dp", "seq", None),
            P("dp", "seq", None),
            P("dp", "seq", None),
            P("dp", None, None),
            P(("dp", "seq"), None),
            P("dp", "seq", None),
        ),
        out_specs=(
            P("dp", "seq", None),
            P("dp", "seq", None),
            P("dp", "seq", None),
            P("dp", "seq", None),
        ),
        check_vma=False,
    )
```

profile of v0, /device:TPU:0, one launch (start us, length us, event | category | flops | bytes accessed | tf_op | source)
XLA Modules:
  0.0 234.0 jit_solution(6987228526842534962)
XLA Ops:
  9.0 6.0 %collective-permute-start.5 = (bf16[256,512]{0,1:T(8,128)(2,1)S(1)}, bf16[256,512]{0,1:T(8,128)(2,1)S(1)}, u32[]{:S(2)}, u32[]{:S(2)}) collective-permute-start(bf16[256,512]{0,1:T(8,128)(2,1)S(1)} %bitcast.364), channel_id=1, source_target_pairs={{0,4},{1,5},{2,6},{3,7},{8,12},{9,13},{10,14},{11,15},{16,20},{17,... | collective-permute-start | bytes 786440 | tf_op jit(solution)/shard_map/ppermute | solution.py:15
  15.0 4.2 %collective-permute-start.4 = (bf16[256,512]{0,1:T(8,128)(2,1)S(1)}, bf16[256,512]{0,1:T(8,128)(2,1)}, u32[]{:S(2)}, u32[]{:S(2)}) collective-permute-start(bf16[256,512]{0,1:T(8,128)(2,1)S(1)} %bitcast.365), channel_id=1, source_target_pairs={{0,2},{1,3},{2,4},{3,5},{4,6},{5,7},{8,10},{9,11},{10,12},{11,13},... | collective-permute-start | bytes 786440 | tf_op jit(solution)/shard_map/ppermute | solution.py:15
  19.2 3.4 %collective-permute-start.3 = (bf16[256,512]{0,1:T(8,128)(2,1)S(1)}, bf16[256,512]{0,1:T(8,128)(2,1)S(1)}, u32[]{:S(2)}, u32[]{:S(2)}) collective-permute-start(bf16[256,512]{0,1:T(8,128)(2,1)S(1)} %bitcast.366), channel_id=1, source_target_pairs={{0,1},{1,2},{2,3},{3,4},{4,5},{5,6},{6,7},{8,9},{9,10},{10,11},{11... | collective-permute-start | bytes 786440 | tf_op jit(solution)/shard_map/ppermute | solution.py:15
  22.6 2.0 collective-permute-start.2
  24.6 2.0 collective-permute-start.1
  26.6 1.3 fusion.50
  28.0 1.4 constant_dynamic-slice_fusion
  34.4 1.5 copy.71
  35.9 2.6 %collective-permute-start = (bf16[256,512]{1,0:T(8,128)(2,1)}, bf16[256,512]{1,0:T(8,128)(2,1)}, u32[]{:S(2)}, u32[]{:S(2)}) collective-permute-start(bf16[256,512]{1,0:T(8,128)(2,1)} %bitcast.9), channel_id=1, source_target_pairs={{0,1},{1,2},{2,3},{3,4},{4,5},{5,6},{6,7},{8,9},{9,10},{10,11},{11... | collective-permute-start | bytes 786440 | tf_op jit(solution)/shard_map/ppermute | solution.py:15
  48.6 2.5 %fusion.92 = (f32[4,256]{1,0:T(4,128)S(1)}, f32[4,256,640]{1,2,0:T(8,128)}) fusion(pred[256,640]{0,1:T(8,128)(4,1)S(1)} %copy-done.44, bf16[256,4,4,128]{0,3,2,1:T(8,128)(2,1)S(1)} %bitcast.353, bf16[640,4,128]{2,0,1:T(8,128)(2,1)S(1)} %pad_maximum_fusion.5), kind=kOutput, calls=%fused_computation.181 | convolution fusion | flops 170394240 | bytes 3215360 | tf_op jit(solution)/shard_map/sub | solution.py:73
  51.1 2.4 %fusion.93 = (f32[4,256]{1,0:T(4,128)S(1)}, f32[4,256,640]{1,2,0:T(8,128)}) fusion(pred[256,640]{0,1:T(8,128)(4,1)S(1)} %copy-done.44, bf16[256,4,4,128]{0,3,2,1:T(8,128)(2,1)S(1)} %bitcast.354, bf16[640,4,128]{2,0,1:T(8,128)(2,1)S(1)} %pad_maximum_fusion.5), kind=kOutput, calls=%fused_computation.182 | convolution fusion | flops 170394240 | bytes 3215360 | tf_op jit(solution)/shard_map/sub | solution.py:73
  53.5 2.5 %fusion.90 = (f32[4,256]{1,0:T(4,128)S(1)}, f32[4,256,640]{1,2,0:T(8,128)}) fusion(pred[256,640]{0,1:T(8,128)(4,1)S(1)} %copy-done.44, bf16[256,4,4,128]{0,3,2,1:T(8,128)(2,1)S(1)} %bitcast.355, bf16[640,4,128]{2,0,1:T(8,128)(2,1)S(1)} %pad_maximum_fusion.5), kind=kOutput, calls=%fused_computation.179 | convolution fusion | flops 170394240 | bytes 3215360 | tf_op jit(solution)/shard_map/sub | solution.py:73
  56.1 2.5 %fusion.91 = (f32[4,256]{1,0:T(4,128)S(1)}, f32[4,256,640]{1,2,0:T(8,128)}) fusion(pred[256,640]{0,1:T(8,128)(4,1)S(1)} %copy-done.44, bf16[256,4,4,128]{0,3,2,1:T(8,128)(2,1)S(1)} %bitcast.356, bf16[640,4,128]{2,0,1:T(8,128)(2,1)S(1)} %pad_maximum_fusion.5), kind=kOutput, calls=%fused_computation.180 | convolution fusion | flops 170394240 | bytes 3215360 | tf_op jit(solution)/shard_map/sub | solution.py:73
  58.5 3.2 %fusion.46 = bf16[4,256,640]{1,2,0:T(8,128)(2,1)} fusion(f32[4,256,640]{1,2,0:T(8,128)} %get-tuple-element.33, f32[4,256]{1,0:T(4,128)S(1)} %get-tuple-element.32), kind=kLoop, calls=%fused_computation.82 | loop fusion | flops 1310720 | bytes 3936256 | tf_op jit(solution)/shard_map/convert_element_type | solution.py:75
  61.7 1.3 fusion.45
  64.0 1.3 fusion.48
  66.4 39.2 %all-gather.2.cloned.1.call-done = bf16[2048,2048]{1,0:T(8,128)(2,1)} async-done(((bf16[64,2048]{1,0:T(8,128)(2,1)}), bf16[2048,2048]{1,0:T(8,128)(2,1)}) %all-gather.2.cloned.1.call-update) | async-done | bytes 8388624 | tf_op jit(solution)/shard_map/all_gather | solution.py:49
  105.6 6.7 %convolution_convert_fusion = bf16[256,2048]{1,0:T(8,128)(2,1)} fusion(bf16[2048,2048]{1,0:T(8,128)(2,1)} %all-gather.2.cloned.1.call-done, bf16[1,256,2048]{2,1,0:T(8,128)(2,1)S(1)} %copy-done), kind=kOutput, calls=%fused_computation.24 | convolution fusion | flops 2148007936 | bytes 10485760 | tf_op jit(solution)/shard_map/dot_general | solution.py:50
  112.3 1.8 reshape.144
  116.5 2.1 copy.142
  118.7 2.8 %convolution_bitcast_fusion.2 = f32[640,1,128]{0,2,1:T(8,128)} fusion(bf16[4,256,640]{1,2,0:T(8,128)(2,1)} %fusion.46, bf16[256,1,4,128]{3,2,1,0:T(4,128)(2,1)} %copy-done.27), kind=kOutput, calls=%fused_computation.63 | convolution fusion | flops 167772160 | bytes 1900544 | tf_op jit(solution)/shard_map/gts,tgd->sd/dot_general | solution.py:97
  121.5 2.1 multiply_reduce_fusion.2
  124.2 2.1 fusion.43
  127.6 2.0 copy.133
  129.6 2.8 %convolution_bitcast_fusion.3 = f32[640,1,128]{0,2,1:T(8,128)} fusion(bf16[4,256,640]{1,2,0:T(8,128)(2,1)} %fusion.45, bf16[256,1,4,128]{3,2,1,0:T(4,128)(2,1)} %copy-done.26), kind=kOutput, calls=%fused_computation.64 | convolution fusion | flops 167772160 | bytes 1900544 | tf_op jit(solution)/shard_map/gts,tgd->sd/dot_general | solution.py:97
  132.4 2.2 multiply_reduce_fusion.3
  134.7 1.6 fusion.11
  136.2 2.0 fusion.44
  140.6 2.0 copy.160
  142.6 2.8 %convolution_bitcast_fusion = f32[640,1,128]{0,2,1:T(8,128)} fusion(bf16[4,256,640]{1,2,0:T(8,128)(2,1)} %fusion.48, bf16[256,1,4,128]{3,2,1,0:T(4,128)(2,1)} %get-tuple-element.21), kind=kOutput, calls=%fused_computation.61 | convolution fusion | flops 167772160 | bytes 1900544 | tf_op jit(solution)/shard_map/gts,tgd->sd/dot_general | solution.py:97
  145.4 2.2 multiply_reduce_fusion
  147.6 1.6 fusion.5
  149.2 2.0 fusion.41
  152.5 2.0 copy.151
  154.6 2.4 %convolution_bitcast_fusion.1 = f32[640,1,128]{0,2,1:T(8,128)} fusion(bf16[4,256,640]{1,2,0:T(8,128)(2,1)S(1)} %fusion.47, bf16[256,1,4,128]{3,2,1,0:T(4,128)(2,1)} %get-tuple-element.19), kind=kOutput, calls=%fused_computation.62 | convolution fusion | flops 167772160 | bytes 1900544 | tf_op jit(solution)/shard_map/gts,tgd->sd/dot_general | solution.py:97
  157.0 2.2 multiply_reduce_fusion.1
  160.2 2.1 fusion.42
  165.3 1.4 collective-permute-start.6
  167.7 1.8 copy.118
  171.0 6.7 %fusion.12 = bf16[1,256,2048]{2,1,0:T(8,128)(2,1)} fusion(bf16[256,2048]{0,1:T(8,128)(2,1)S(1)} %bitcast.351, bf16[2048,2048]{1,0:T(8,128)(2,1)} %all-gather.2.cloned.1.call-done), kind=kOutput, calls=%fused_computation.26 | convolution fusion | flops 2148007936 | bytes 10485760 | tf_op jit(solution)/shard_map/dot_general | solution.py:104
  179.5 1.4 copy.122
  182.9 1.4 collective-permute-start.7
  184.3 1.3 collective-permute-start.8
  187.4 1.3 collective-permute-start.11
  190.7 6.3 %collective-permute-done.7 = f32[128,512]{1,0:T(8,128)} collective-permute-done((f32[128,512]{1,0:T(8,128)}, f32[128,512]{1,0:T(8,128)}, u32[]{:S(2)}, u32[]{:S(2)}) %collective-permute-start.7) | collective-permute-done | bytes 262176 | tf_op jit(solution)/shard_map/ppermute | solution.py:15
  198.1 5.3 %collective-permute-done.10 = f32[128,512]{1,0:T(8,128)S(1)} collective-permute-done((f32[128,512]{1,0:T(8,128)S(1)}, f32[128,512]{1,0:T(8,128)S(1)}, u32[]{:S(2)}, u32[]{:S(2)}) %collective-permute-start.10) | collective-permute-done | bytes 262176 | tf_op jit(solution)/shard_map/ppermute | solution.py:15
  203.5 8.4 %collective-permute-done.8 = f32[128,512]{1,0:T(8,128)} collective-permute-done((f32[128,512]{1,0:T(8,128)S(1)}, f32[128,512]{1,0:T(8,128)}, u32[]{:S(2)}, u32[]{:S(2)}) %collective-permute-start.8) | collective-permute-done | bytes 262176 | tf_op jit(solution)/shard_map/ppermute | solution.py:15
  213.6 12.8 %collective-permute-done.11 = f32[128,512]{1,0:T(8,128)S(1)} collective-permute-done((f32[128,512]{1,0:T(8,128)S(1)}, f32[128,512]{1,0:T(8,128)S(1)}, u32[]{:S(2)}, u32[]{:S(2)}) %collective-permute-start.11) | collective-permute-done | bytes 262176 | tf_op jit(solution)/shard_map/ppermute | solution.py:15
  (156 shorter events, 40.3 us)
Async XLA Ops:
  7.2 98.5 %copy-start = (bf16[1,256,2048]{2,1,0:T(8,128)(2,1)S(1)}, bf16[1,256,2048]{2,1,0:T(8,128)(2,1)}, u32[]{:S(2)}) copy-start(bf16[1,256,2048]{2,1,0:T(8,128)(2,1)} %param.11) | copy-start | bytes 3145732
  7.2 98.4 %all-gather.2.cloned.1.call-start = ((), (), s32[]{:S(2)}) async-start(), calls=%async_computation | async-start | bytes 8650752 | tf_op jit(solution)/shard_map/all_gather | solution.py:49
  9.0 26.9 %collective-permute-start.5 = (bf16[256,512]{0,1:T(8,128)(2,1)S(1)}, bf16[256,512]{0,1:T(8,128)(2,1)S(1)}, u32[]{:S(2)}, u32[]{:S(2)}) collective-permute-start(bf16[256,512]{0,1:T(8,128)(2,1)S(1)} %bitcast.364), channel_id=1, source_target_pairs={{0,4},{1,5},{2,6},{3,7},{8,12},{9,13},{10,14},{11,15},{16,20},{17,... | collective-permute-start | bytes 786440 | tf_op jit(solution)/shard_map/ppermute | solution.py:15
  15.0 23.6 %collective-permute-start.4 = (bf16[256,512]{0,1:T(8,128)(2,1)S(1)}, bf16[256,512]{0,1:T(8,128)(2,1)}, u32[]{:S(2)}, u32[]{:S(2)}) collective-permute-start(bf16[256,512]{0,1:T(8,128)(2,1)S(1)} %bitcast.365), channel_id=1, source_target_pairs={{0,2},{1,3},{2,4},{3,5},{4,6},{5,7},{8,10},{9,11},{10,12},{11,13},... | collective-permute-start | bytes 786440 | tf_op jit(solution)/shard_map/ppermute | solution.py:15
  19.2 20.3 %collective-permute-start.3 = (bf16[256,512]{0,1:T(8,128)(2,1)S(1)}, bf16[256,512]{0,1:T(8,128)(2,1)S(1)}, u32[]{:S(2)}, u32[]{:S(2)}) collective-permute-start(bf16[256,512]{0,1:T(8,128)(2,1)S(1)} %bitcast.366), channel_id=1, source_target_pairs={{0,1},{1,2},{2,3},{3,4},{4,5},{5,6},{6,7},{8,9},{9,10},{10,11},{11... | collective-permute-start | bytes 786440 | tf_op jit(solution)/shard_map/ppermute | solution.py:15
  22.6 18.0 %collective-permute-start.2 = (bf16[256,512]{1,0:T(8,128)(2,1)}, bf16[256,512]{1,0:T(8,128)(2,1)}, u32[]{:S(2)}, u32[]{:S(2)}) collective-permute-start(bf16[256,512]{1,0:T(8,128)(2,1)} %bitcast.9), channel_id=1, source_target_pairs={{0,4},{1,5},{2,6},{3,7},{8,12},{9,13},{10,14},{11,15},{16,20},{17,... | collective-permute-start | bytes 786440 | tf_op jit(solution)/shard_map/ppermute | solution.py:15
  24.6 18.5 %collective-permute-start.1 = (bf16[256,512]{1,0:T(8,128)(2,1)}, bf16[256,512]{1,0:T(8,128)(2,1)}, u32[]{:S(2)}, u32[]{:S(2)}) collective-permute-start(bf16[256,512]{1,0:T(8,128)(2,1)} %bitcast.9), channel_id=1, source_target_pairs={{0,2},{1,3},{2,4},{3,5},{4,6},{5,7},{8,10},{9,11},{10,12},{11,13},... | collective-permute-start | bytes 786440 | tf_op jit(solution)/shard_map/ppermute | solution.py:15
  35.9 20.2 %copy-start.4 = (bf16[1,256,2048]{1,2,0:T(8,128)(2,1)}, bf16[1,256,2048]{1,2,0:T(8,128)(2,1)S(1)}, u32[]{:S(2)}) copy-start(bf16[1,256,2048]{1,2,0:T(8,128)(2,1)S(1)} %copy.71) | copy-start | bytes 3145732
  35.9 8.8 %collective-permute-start = (bf16[256,512]{1,0:T(8,128)(2,1)}, bf16[256,512]{1,0:T(8,128)(2,1)}, u32[]{:S(2)}, u32[]{:S(2)}) collective-permute-start(bf16[256,512]{1,0:T(8,128)(2,1)} %bitcast.9), channel_id=1, source_target_pairs={{0,1},{1,2},{2,3},{3,4},{4,5},{5,6},{6,7},{8,9},{9,10},{10,11},{11... | collective-permute-start | bytes 786440 | tf_op jit(solution)/shard_map/ppermute | solution.py:15
  47.5 8.6 %copy-start.22 = (bf16[640,4,128]{2,0,1:T(8,128)(2,1)}, bf16[640,4,128]{2,0,1:T(8,128)(2,1)S(1)}, u32[]{:S(2)}) copy-start(bf16[640,4,128]{2,0,1:T(8,128)(2,1)S(1)} %pad_maximum_fusion.5) | copy-start | bytes 1966084
  58.5 3.2 %copy-start.19 = (f32[4,256,640]{1,2,0:T(8,128)S(1)}, f32[4,256,640]{1,2,0:T(8,128)}, u32[]{:S(2)}) copy-start(f32[4,256,640]{1,2,0:T(8,128)} %get-tuple-element.35) | copy-start | bytes 7864324
  61.7 2.2 copy-start.17
  64.0 2.2 copy-start.15
  116.5 5.0 %copy-start.13 = (bf16[640,4,128]{0,2,1:T(8,128)(2,1)S(1)}, bf16[640,4,128]{0,2,1:T(8,128)(2,1)}, u32[]{:S(2)}) copy-start(bf16[640,4,128]{0,2,1:T(8,128)(2,1)} %pad_maximum_fusion.4) | copy-start | bytes 1966084
  116.5 7.1 %copy-start.28 = (bf16[256,1,4,128]{3,2,1,0:T(4,128)(2,1)S(1)}, bf16[256,1,4,128]{3,2,1,0:T(4,128)(2,1)}, u32[]{:S(2)}) copy-start(bf16[256,1,4,128]{3,2,1,0:T(4,128)(2,1)} %copy-done.27) | copy-start | bytes 786436
  118.7 2.8 %copy-start.3 = (bf16[4,256,640]{1,2,0:T(8,128)(2,1)S(1)}, bf16[4,256,640]{1,2,0:T(8,128)(2,1)}, u32[]{:S(2)}) copy-start(bf16[4,256,640]{1,2,0:T(8,128)(2,1)} %fusion.46) | copy-start | bytes 3932164
  118.7 4.9 %copy-start.21 = (f32[4,256,640]{1,2,0:T(8,128)S(1)}, f32[4,256,640]{1,2,0:T(8,128)}, u32[]{:S(2)}) copy-start(f32[4,256,640]{1,2,0:T(8,128)} %get-tuple-element.33) | copy-start | bytes 7864324
  124.1 2.1 copy-start.5
  129.6 2.8 %copy-start.2 = (bf16[4,256,640]{1,2,0:T(8,128)(2,1)S(1)}, bf16[4,256,640]{1,2,0:T(8,128)(2,1)}, u32[]{:S(2)}) copy-start(bf16[4,256,640]{1,2,0:T(8,128)(2,1)} %fusion.45) | copy-start | bytes 3932164
  129.6 5.1 %copy-start.20 = (f32[4,256,640]{1,2,0:T(8,128)S(1)}, f32[4,256,640]{1,2,0:T(8,128)}, u32[]{:S(2)}) copy-start(f32[4,256,640]{1,2,0:T(8,128)} %get-tuple-element.35) | copy-start | bytes 7864324
  142.6 2.8 %copy-start.1 = (bf16[4,256,640]{1,2,0:T(8,128)(2,1)S(1)}, bf16[4,256,640]{1,2,0:T(8,128)(2,1)}, u32[]{:S(2)}) copy-start(bf16[4,256,640]{1,2,0:T(8,128)(2,1)} %fusion.48) | copy-start | bytes 3932164
  142.6 5.0 %copy-start.18 = (f32[4,256,640]{1,2,0:T(8,128)S(1)}, f32[4,256,640]{1,2,0:T(8,128)}, u32[]{:S(2)}) copy-start(f32[4,256,640]{1,2,0:T(8,128)} %get-tuple-element.29) | copy-start | bytes 7864324
  154.6 2.4 %copy-start.14 = (bf16[640,4,128]{0,2,1:T(8,128)(2,1)S(1)}, bf16[640,4,128]{0,2,1:T(8,128)(2,1)}, u32[]{:S(2)}) copy-start(bf16[640,4,128]{0,2,1:T(8,128)(2,1)} %pad_maximum_fusion.4) | copy-start | bytes 1966084
  154.6 4.6 %copy-start.16 = (f32[4,256,640]{1,2,0:T(8,128)S(1)}, f32[4,256,640]{1,2,0:T(8,128)}, u32[]{:S(2)}) copy-start(f32[4,256,640]{1,2,0:T(8,128)} %get-tuple-element.31) | copy-start | bytes 7864324
  157.0 2.2 copy-start.24
  160.2 2.1 copy-start.9
  160.2 2.1 copy-start.11
  160.2 2.1 copy-start.12
  163.3 3.5 %copy-start.6 = (f32[640,1,128]{0,2,1:T(8,128)S(1)}, f32[640,1,128]{0,2,1:T(8,128)}, u32[]{:S(2)}) copy-start(f32[640,1,128]{0,2,1:T(8,128)} %convolution_bitcast_fusion.2) | copy-start | bytes 983044
  163.3 3.5 %copy-start.7 = (f32[640,1,128]{0,2,1:T(8,128)S(1)}, f32[640,1,128]{0,2,1:T(8,128)}, u32[]{:S(2)}) copy-start(f32[640,1,128]{0,2,1:T(8,128)} %convolution_bitcast_fusion.3) | copy-start | bytes 983044
  163.3 3.5 %copy-start.8 = (f32[640,1,128]{0,2,1:T(8,128)S(1)}, f32[640,1,128]{0,2,1:T(8,128)}, u32[]{:S(2)}) copy-start(f32[640,1,128]{0,2,1:T(8,128)} %convolution_bitcast_fusion) | copy-start | bytes 983044
  163.3 3.5 %copy-start.10 = (f32[640,1,128]{0,2,1:T(8,128)S(1)}, f32[640,1,128]{0,2,1:T(8,128)}, u32[]{:S(2)}) copy-start(f32[640,1,128]{0,2,1:T(8,128)} %convolution_bitcast_fusion.1) | copy-start | bytes 983044
  165.3 5.5 %copy-start.29 = (bf16[128,4,256]{2,0,1:T(8,128)(2,1)S(1)}, bf16[128,4,256]{2,0,1:T(8,128)(2,1)}, u32[]{:S(2)}) copy-start(bf16[128,4,256]{2,0,1:T(8,128)(2,1)} %get-tuple-element.41) | copy-start | bytes 786436
  165.3 5.5 %copy-start.30 = (bf16[128,4,256]{2,0,1:T(8,128)(2,1)S(1)}, bf16[128,4,256]{2,0,1:T(8,128)(2,1)}, u32[]{:S(2)}) copy-start(bf16[128,4,256]{2,0,1:T(8,128)(2,1)} %get-tuple-element.43) | copy-start | bytes 786436
  165.3 5.5 %copy-start.31 = (bf16[128,4,256]{2,0,1:T(8,128)(2,1)S(1)}, bf16[128,4,256]{2,0,1:T(8,128)(2,1)}, u32[]{:S(2)}) copy-start(bf16[128,4,256]{2,0,1:T(8,128)(2,1)} %get-tuple-element.37) | copy-start | bytes 786436
  165.3 5.5 %copy-start.32 = (bf16[128,4,256]{2,0,1:T(8,128)(2,1)S(1)}, bf16[128,4,256]{2,0,1:T(8,128)(2,1)}, u32[]{:S(2)}) copy-start(bf16[128,4,256]{2,0,1:T(8,128)(2,1)} %get-tuple-element.39) | copy-start | bytes 786436
  165.3 22.1 %collective-permute-start.6 = (f32[128,512]{1,0:T(8,128)}, f32[128,512]{1,0:T(8,128)}, u32[]{:S(2)}, u32[]{:S(2)}) collective-permute-start(f32[128,512]{1,0:T(8,128)} %copy.105), channel_id=1, source_target_pairs={{1,0},{2,1},{3,2},{4,3},{5,4},{6,5},{7,6},{9,8},{10,9},{11,10},{12... | collective-permute-start | bytes 786440 | tf_op jit(solution)/shard_map/ppermute | solution.py:15
  169.5 20.2 %collective-permute-start.9 = (f32[128,512]{1,0:T(8,128)}, f32[128,512]{1,0:T(8,128)}, u32[]{:S(2)}, u32[]{:S(2)}) collective-permute-start(f32[128,512]{1,0:T(8,128)} %copy.118), channel_id=1, source_target_pairs={{1,0},{2,1},{3,2},{4,3},{5,4},{6,5},{7,6},{9,8},{10,9},{11,10},{12... | collective-permute-start | bytes 786440 | tf_op jit(solution)/shard_map/ppermute | solution.py:15
  177.7 1.4 copy-start.39
  177.7 1.7 copy-start.40
  179.5 1.4 slice-start
  181.1 4.5 %slice-start.1 = ((f32[640,4,128]{0,2,1:T(8,128)}), f32[256,4,128]{0,2,1:T(8,128)S(1)}, s32[]{:S(2)}) async-start(f32[640,4,128]{0,2,1:T(8,128)} %pad_maximum_fusion.1), calls=%async_computation.2 | async-start | bytes 1048576 | tf_op jit(solution)/shard_map/slice | solution.py:107
  182.0 3.8 %copy-start.34 = (f32[128,4,128]{0,2,1:T(8,128)S(1)}, f32[128,4,128]{0,2,1:T(8,128)}, u32[]{:S(2)}) copy-start(f32[128,4,128]{0,2,1:T(8,128)} %get-tuple-element.12) | copy-start | bytes 786436
  182.9 3.1 %copy-start.33 = (f32[128,4,128]{0,2,1:T(8,128)S(1)}, f32[128,4,128]{0,2,1:T(8,128)}, u32[]{:S(2)}) copy-start(f32[128,4,128]{0,2,1:T(8,128)} %get-tuple-element.13) | copy-start | bytes 786436
  182.9 14.2 %collective-permute-start.7 = (f32[128,512]{1,0:T(8,128)}, f32[128,512]{1,0:T(8,128)}, u32[]{:S(2)}, u32[]{:S(2)}) collective-permute-start(f32[128,512]{1,0:T(8,128)} %copy.107), channel_id=1, source_target_pairs={{2,0},{3,1},{4,2},{5,3},{6,4},{7,5},{10,8},{11,9},{12,10},{13,11},... | collective-permute-start | bytes 786440 | tf_op jit(solution)/shard_map/ppermute | solution.py:15
  184.3 27.6 %collective-permute-start.8 = (f32[128,512]{1,0:T(8,128)S(1)}, f32[128,512]{1,0:T(8,128)}, u32[]{:S(2)}, u32[]{:S(2)}) collective-permute-start(f32[128,512]{1,0:T(8,128)S(1)} %copy.108), channel_id=1, source_target_pairs={{4,0},{5,1},{6,2},{7,3},{12,8},{13,9},{14,10},{15,11},{20,16},{21,... | collective-permute-start | bytes 786440 | tf_op jit(solution)/shard_map/ppermute | solution.py:15
  186.1 17.3 %collective-permute-start.10 = (f32[128,512]{1,0:T(8,128)S(1)}, f32[128,512]{1,0:T(8,128)S(1)}, u32[]{:S(2)}, u32[]{:S(2)}) collective-permute-start(f32[128,512]{1,0:T(8,128)S(1)} %copy.120), channel_id=1, source_target_pairs={{2,0},{3,1},{4,2},{5,3},{6,4},{7,5},{10,8},{11,9},{12,10},{13,11},... | collective-permute-start | bytes 786440 | tf_op jit(solution)/shard_map/ppermute | solution.py:15
  187.4 39.0 %collective-permute-start.11 = (f32[128,512]{1,0:T(8,128)S(1)}, f32[128,512]{1,0:T(8,128)S(1)}, u32[]{:S(2)}, u32[]{:S(2)}) collective-permute-start(f32[128,512]{1,0:T(8,128)S(1)} %copy.121), channel_id=1, source_target_pairs={{4,0},{5,1},{6,2},{7,3},{12,8},{13,9},{14,10},{15,11},{20,16},{21,... | collective-permute-start | bytes 786440 | tf_op jit(solution)/shard_map/ppermute | solution.py:15
  (12 other events, 13.7 us)
Sparse Core Ops, SparseCore 0:
  11.0 94.5 all-gather.1
where the time goes:
time: 235 us; the launch traced here: 234 us
  waiting for transfers between devices  73.5 us (31%)
  matrix products  59.8 us (25%)
  local copies, waits for them, and re-layouts  32.5 us (14%)
  starting transfers between devices  28.3 us (12%)
  other arithmetic  21.5 us (9%)
  between operations  18.4 us (8%)
    all_gather x1, waiting for transfers between devices, shards(): whole_weight = lax.all_gather(out_weight, ('dp', 'seq'), axis=0, tiled=True)  39.2 us
    ppermute x12, waiting for transfers between devices, shifted(): return lax.ppermute(block, axis, route)  33.7 us
    ppermute x12, starting transfers between devices, shifted(): return lax.ppermute(block, axis, route)  28.2 us
    unnamed x98, local copies, waits for them, and re-layouts  16.7 us
    dot_general x4, matrix products, shards(): jnp.einsum('gts,tgd->sd', probs_low, grad_group, preferred_element_type=j...  10.9 us
    sub x4, matrix products, shards(): exp_scores = jnp.exp(scores - row_max)  9.91 us
    dot_general x4, matrix products, shards(): jnp.einsum('gts,sd->tgd', probs_low, value_group, preferred_element_type=...  8.71 us
    dot_general x4, matrix products, shards(): jnp.einsum('gts,sd->tgd', score_low, key_group, preferred_element_type=jn...  8.28 us
  transfers between devices with their start and end apart: 13, of which 6 were waited for; matrix products, arithmetic and copies ran while one was open for 21% of the time, Pallas kernels for 0%

commit v1 on v0

--- a/solution.py
+++ b/solution.py
@@ -46,7 +46,17 @@
     far_level = jnp.maximum(col_ids - tok_count, 0) // BLOCK
     far_seen = shard_index >= jnp.left_shift(jnp.int32(1), far_level)
     visible = jnp.where(col_ids < tok_count, col_ids <= row_ids, far_seen)
-    whole_weight = lax.all_gather(out_weight, ("dp", "seq"), axis=0, tiled=True)
+    z, vec_out = (jax.lax.axis_size(("dp", "seq")), jax.lax.axis_index(("dp", "seq")))
+    whole_weight, next_value = (out_weight, 1)
+    while next_value < z:
+        steps_seen = []
+        for q in range(z):
+            steps_seen.append((q, q ^ next_value))
+        tile_out = jax.lax.ppermute(whole_weight, ("dp", "seq"), steps_seen)
+        heard = jnp.concatenate([whole_weight, tile_out], 0)
+        oldest = jnp.concatenate([tile_out, whole_weight], 0)
+        whole_weight = jnp.where(vec_out & next_value == 0, heard, oldest)
+        next_value = 2 * next_value
     attn_grad = lax.dot_general(
         grad_rows, whole_weight, (((1,), (1,)), ((), ())), preferred_element_type=jnp.float32
     )

time: 235 us -> 318 us (1.35)
  waiting for transfers between devices: 73.5 us -> 140 us
  other arithmetic: 21.5 us -> 37.5 us
  between operations: 18.4 us -> 5.12 us
  starting transfers between devices: 28.3 us -> 35.8 us
  local copies, waits for them, and re-layouts: 32.5 us -> 37.4 us
    ppermute x0 -> x5, waiting for transfers between devices: none -> 110 us  [shards(): tile_out = jax.lax.ppermute(whole_weight, ('dp', 'seq'), steps_seen)]
    all_gather x1 -> x0, waiting for transfers between devices: 39.2 us -> none  [shards(): whole_weight = lax.all_gather(out_weight, ('dp', 'seq'), axis=0, tiled=True)]
    select_n x0 -> x4, other arithmetic: none -> 9.69 us  [shards(): whole_weight = jnp.where(vec_out & next_value == 0, heard, oldest)]
    ppermute x0 -> x5, starting transfers between devices: none -> 9.01 us  [shards(): tile_out = jax.lax.ppermute(whole_weight, ('dp', 'seq'), steps_seen)]
    dot_general x4, matrix products: 10.9 us -> 2.12 us  [shards(): jnp.einsum('gts,tgd->sd', probs_low, grad_group, preferred_element_type=j...]
    unnamed x98 -> x76, local copies, waits for them, and re-layouts: 16.7 us -> 22.3 us
    dot_general x4, matrix products: 4.2 us -> 9.43 us  [shards(): jnp.einsum('tgd,sd->gts', grad_group, value_group, preferred_element_type...]
    unnamed x2 -> x4, other arithmetic: 2.21 us -> 7.11 us
  transfers between devices with their start and end apart: 13 -> 17, of which waited for: 6 -> 8; matrix products, arithmetic and copies ran while one was open for 21% -> 19% of each run, Pallas kernels for 0% -> 0%
where the time goes in v1:
time: 318 us; the launch traced here: 316 us
  waiting for transfers between devices  140 us (44%)
  matrix products  60.7 us (19%)
  other arithmetic  37.5 us (12%)
  local copies, waits for them, and re-layouts  37.4 us (12%)
  starting transfers between devices  35.8 us (11%)
  between operations  5.12 us (2%)
    ppermute x5, waiting for transfers between devices, shards(): tile_out = jax.lax.ppermute(whole_weight, ('dp', 'seq'), steps_seen)  110 us
    ppermute x12, waiting for transfers between devices, shifted(): return lax.ppermute(block, axis, route)  29.8 us
    ppermute x12, starting transfers between devices, shifted(): return lax.ppermute(block, axis, route)  26.8 us
    unnamed x76, local copies, waits for them, and re-layouts  22.3 us
    sub x4, matrix products, shards(): exp_scores = jnp.exp(scores - row_max)  11 us
    dot_general x4, matrix products, shards(): jnp.einsum('gts,sd->tgd', probs_low, value_group, preferred_element_type=...  9.9 us
    select_n x4, other arithmetic, shards(): whole_weight = jnp.where(vec_out & next_value == 0, heard, oldest)  9.69 us
    dot_general x4, matrix products, shards(): jnp.einsum('tgd,sd->gts', grad_group, value_group, preferred_element_type...  9.43 us
  transfers between devices with their start and end apart: 17, of which 8 were waited for; matrix products, arithmetic and copies ran while one was open for 19% of the time, Pallas kernels for 0%

profile of v1, /device:TPU:0, one launch (start us, length us, event | category | flops | bytes accessed | tf_op | source)
XLA Modules:
  0.0 316.2 jit_solution(12492255793993567572)
XLA Ops:
  0.6 3.0 collective-permute-start.6
  3.7 6.5 %collective-permute-done.6 = bf16[64,2048]{1,0:T(8,128)(2,1)S(1)} collective-permute-done((bf16[64,2048]{1,0:T(8,128)(2,1)}, bf16[64,2048]{1,0:T(8,128)(2,1)S(1)}, u32[]{:S(2)}, u32[]{:S(2)}) %collective-permute-start.6) | collective-permute-done | bytes 262176 | tf_op jit(solution)/shard_map/ppermute | solution.py:55
  11.3 1.9 collective-permute-start.7
  13.2 11.3 %collective-permute-done.7 = bf16[128,2048]{1,0:T(8,128)(2,1)S(1)} collective-permute-done((bf16[128,2048]{1,0:T(8,128)(2,1)S(1)}, bf16[128,2048]{1,0:T(8,128)(2,1)S(1)}, u32[]{:S(2)}, u32[]{:S(2)}) %collective-permute-start.7) | collective-permute-done | bytes 524320 | tf_op jit(solution)/shard_map/ppermute | solution.py:55
  24.8 2.6 collective-permute-start.8
  27.4 44.4 %collective-permute-done.8 = bf16[256,2048]{1,0:T(8,128)(2,1)} collective-permute-done((bf16[256,2048]{1,0:T(8,128)(2,1)S(1)}, bf16[256,2048]{1,0:T(8,128)(2,1)}, u32[]{:S(2)}, u32[]{:S(2)}) %collective-permute-start.8) | collective-permute-done | bytes 1048608 | tf_op jit(solution)/shard_map/ppermute | solution.py:55
  71.8 3.1 maximum_select_fusion.2
  75.8 2.1 collective-permute-start.5
  77.9 6.8 %collective-permute-start.4 = (bf16[256,512]{0,1:T(8,128)(2,1)}, bf16[256,512]{0,1:T(8,128)(2,1)}, u32[]{:S(2)}, u32[]{:S(2)}) collective-permute-start(bf16[256,512]{0,1:T(8,128)(2,1)} %bitcast.19), channel_id=1, source_target_pairs={{0,2},{1,3},{2,4},{3,5},{4,6},{5,7},{8,10},{9,11},{10,12},{11,13},... | collective-permute-start | bytes 786440 | tf_op jit(solution)/shard_map/ppermute | solution.py:15
  84.7 4.1 %collective-permute-start.3 = (bf16[256,512]{0,1:T(8,128)(2,1)}, bf16[256,512]{0,1:T(8,128)(2,1)}, u32[]{:S(2)}, u32[]{:S(2)}) collective-permute-start(bf16[256,512]{0,1:T(8,128)(2,1)} %bitcast.19), channel_id=1, source_target_pairs={{0,1},{1,2},{2,3},{3,4},{4,5},{5,6},{6,7},{8,9},{9,10},{10,11},{11... | collective-permute-start | bytes 786440 | tf_op jit(solution)/shard_map/ppermute | solution.py:15
  88.9 2.0 collective-permute-start.2
  90.9 5.2 %maximum_select_fusion.1 = bf16[1024,2048]{1,0:T(8,128)(2,1)} fusion(bf16[512,2048]{1,0:T(8,128)(2,1)} %collective-permute-done.9, bf16[512,2048]{1,0:T(8,128)(2,1)S(1)} %maximum_select_fusion.2, pred[]{:T(512)S(6)} %eq.16), kind=kLoop, calls=%fused_computation.5 | loop fusion | flops 18874368 | bytes 8388609 | tf_op jit(solution)/shard_map/jit(_where)/select_n | solution.py:58
  106.2 2.0 collective-permute-start.1
  109.1 2.0 collective-permute-start
  120.0 2.2 pad_maximum_fusion.4
  122.2 3.5 %fusion.92 = (f32[4,256]{1,0:T(4,128)S(1)}, f32[4,256,640]{1,2,0:T(8,128)}) fusion(pred[256,640]{0,1:T(8,128)(4,1)} %fusion.50, bf16[256,4,4,128]{0,3,2,1:T(8,128)(2,1)S(1)} %bitcast.361, bf16[640,4,128]{2,0,1:T(8,128)(2,1)S(1)} %pad_maximum_fusion.5), kind=kOutput, calls=%fused_computation.186 | convolution fusion | flops 170394240 | bytes 3215360 | tf_op jit(solution)/shard_map/sub | solution.py:83
  125.7 2.5 fusion.93
  128.1 2.6 fusion.94
  130.7 2.5 fusion.95
  133.2 2.1 fusion.48
  140.7 47.7 %collective-permute-done.10 = bf16[1024,2048]{1,0:T(8,128)(2,1)} collective-permute-done((bf16[1024,2048]{1,0:T(8,128)(2,1)}, bf16[1024,2048]{1,0:T(8,128)(2,1)}, u32[]{:S(2)}, u32[]{:S(2)}) %collective-permute-start.10) | collective-permute-done | bytes 4194336 | tf_op jit(solution)/shard_map/ppermute | solution.py:55
  188.5 7.4 %convolution_convert_fusion = bf16[2048,256]{1,0:T(8,128)(2,1)S(1)} fusion(bf16[1024,2048]{1,0:T(8,128)(2,1)} %collective-permute-done.10, bf16[1024,2048]{1,0:T(8,128)(2,1)} %maximum_select_fusion.1, pred[]{:T(512)S(6)} %eq.15, bf16[1,256,2048]{2,1,0:T(8,128)(2,1)S(1)} %copy-done), kind=kOutput, calls=%fused_computation.26 | convolution fusion | flops 2185756672 | bytes 10485761 | tf_op jit(solution)/shard_map/dot_general | solution.py:60
  197.9 1.9 copy.194
  201.5 2.0 copy.160
  203.6 2.2 multiply_reduce_fusion
  205.8 2.4 fusion.5
  208.1 2.0 fusion.41
  211.4 1.8 copy.193
  215.0 2.0 copy.151
  217.0 2.6 multiply_reduce_fusion.1
  219.6 2.4 fusion.7
  221.9 2.0 fusion.42
  225.2 1.8 copy.192
  228.8 2.0 copy.142
  230.8 2.6 multiply_reduce_fusion.2
  233.4 2.4 fusion.9
  235.7 2.0 fusion.43
  239.0 1.8 copy.191
  242.6 2.0 copy.133
  244.6 2.6 multiply_reduce_fusion.3
  247.2 2.4 fusion.11
  249.6 2.1 fusion.44
  256.8 1.8 copy.105
  263.0 8.3 %fusion.12 = bf16[1,256,2048]{2,1,0:T(8,128)(2,1)} fusion(bf16[256,2048]{0,1:T(8,128)(2,1)S(1)} %bitcast.381, bf16[1024,2048]{1,0:T(8,128)(2,1)} %collective-permute-done.10, bf16[1024,2048]{1,0:T(8,128)(2,1)} %maximum_select_fusion.1, pred[]{:T(512)S(6)} %eq.15), kind=kOutput, calls=%fused_computation.28 | convolution fusion | flops 2185756672 | bytes 10485761 | tf_op jit(solution)/shard_map/dot_general | solution.py:114
  282.9 6.0 %collective-permute-done.12 = f32[128,512]{1,0:T(8,128)} collective-permute-done((f32[128,512]{1,0:T(8,128)S(1)}, f32[128,512]{1,0:T(8,128)}, u32[]{:S(2)}, u32[]{:S(2)}) %collective-permute-start.12) | collective-permute-done | bytes 262176 | tf_op jit(solution)/shard_map/ppermute | solution.py:15
  289.9 3.7 %collective-permute-done.15 = f32[128,512]{1,0:T(8,128)} collective-permute-done((f32[128,512]{1,0:T(8,128)S(1)}, f32[128,512]{1,0:T(8,128)}, u32[]{:S(2)}, u32[]{:S(2)}) %collective-permute-start.15) | collective-permute-done | bytes 262176 | tf_op jit(solution)/shard_map/ppermute | solution.py:15
  294.6 12.5 %collective-permute-done.13 = f32[128,512]{1,0:T(8,128)S(1)} collective-permute-done((f32[128,512]{1,0:T(8,128)S(1)}, f32[128,512]{1,0:T(8,128)S(1)}, u32[]{:S(2)}, u32[]{:S(2)}) %collective-permute-start.13) | collective-permute-done | bytes 262176 | tf_op jit(solution)/shard_map/ppermute | solution.py:15
  307.8 7.6 %collective-permute-done.16 = f32[128,512]{1,0:T(8,128)S(1)} collective-permute-done((f32[128,512]{1,0:T(8,128)S(1)}, f32[128,512]{1,0:T(8,128)S(1)}, u32[]{:S(2)}, u32[]{:S(2)}) %collective-permute-start.16) | collective-permute-done | bytes 262176 | tf_op jit(solution)/shard_map/ppermute | solution.py:15
  (146 shorter events, 60.9 us)
Async XLA Ops:
  0.6 187.9 %copy-start = (bf16[1,256,2048]{2,1,0:T(8,128)(2,1)S(1)}, bf16[1,256,2048]{2,1,0:T(8,128)(2,1)}, u32[]{:S(2)}) copy-start(bf16[1,256,2048]{2,1,0:T(8,128)(2,1)} %param.11) | copy-start | bytes 3145732
  0.6 9.5 %collective-permute-start.6 = (bf16[64,2048]{1,0:T(8,128)(2,1)}, bf16[64,2048]{1,0:T(8,128)(2,1)S(1)}, u32[]{:S(2)}, u32[]{:S(2)}) collective-permute-start(bf16[64,2048]{1,0:T(8,128)(2,1)} %param.10), channel_id=1, source_target_pairs={{0,1},{1,0},{2,3},{3,2},{4,5},{5,4},{6,7},{7,6},{8,9},{9,8},{10,11... | collective-permute-start | bytes 786440 | tf_op jit(solution)/shard_map/ppermute | solution.py:55
  11.3 13.2 %collective-permute-start.7 = (bf16[128,2048]{1,0:T(8,128)(2,1)S(1)}, bf16[128,2048]{1,0:T(8,128)(2,1)S(1)}, u32[]{:S(2)}, u32[]{:S(2)}) collective-permute-start(bf16[128,2048]{1,0:T(8,128)(2,1)S(1)} %maximum_select_fusion.6), channel_id=1, source_target_pairs={{0,2},{1,3},{2,0},{3,1},{4,6},{5,7},{6,4},{7,5},{8,10},{9,11},{10,... | collective-permute-start | bytes 1572872 | tf_op jit(solution)/shard_map/ppermute | solution.py:55
  24.8 2.6 copy-start.5
  24.8 50.2 %copy-start.27 = (bf16[1,256,512]{2,1,0:T(8,128)(2,1)S(1)}, bf16[1,256,512]{2,1,0:T(8,128)(2,1)}, u32[]{:S(2)}) copy-start(bf16[1,256,512]{2,1,0:T(8,128)(2,1)} %param.7) | copy-start | bytes 786436
  24.8 47.0 %collective-permute-start.8 = (bf16[256,2048]{1,0:T(8,128)(2,1)S(1)}, bf16[256,2048]{1,0:T(8,128)(2,1)}, u32[]{:S(2)}, u32[]{:S(2)}) collective-permute-start(bf16[256,2048]{1,0:T(8,128)(2,1)S(1)} %maximum_select_fusion.5), channel_id=1, source_target_pairs={{0,4},{1,5},{2,6},{3,7},{4,0},{5,1},{6,2},{7,3},{8,12},{9,13},{10,... | collective-permute-start | bytes 3145736 | tf_op jit(solution)/shard_map/ppermute | solution.py:55
  74.9 16.0 %collective-permute-start.9 = (bf16[512,2048]{1,0:T(8,128)(2,1)S(1)}, bf16[512,2048]{1,0:T(8,128)(2,1)}, u32[]{:S(2)}, u32[]{:S(2)}) collective-permute-start(bf16[512,2048]{1,0:T(8,128)(2,1)S(1)} %maximum_select_fusion.2), channel_id=1, source_target_pairs={{0,8},{1,9},{2,10},{3,11},{4,12},{5,13},{6,14},{7,15},{8,0},{9,1},... | collective-permute-start | bytes 6291464 | tf_op jit(solution)/shard_map/ppermute | solution.py:55
  75.8 30.3 %collective-permute-start.5 = (bf16[256,512]{0,1:T(8,128)(2,1)}, bf16[256,512]{0,1:T(8,128)(2,1)}, u32[]{:S(2)}, u32[]{:S(2)}) collective-permute-start(bf16[256,512]{0,1:T(8,128)(2,1)} %bitcast.19), channel_id=1, source_target_pairs={{0,4},{1,5},{2,6},{3,7},{8,12},{9,13},{10,14},{11,15},{16,20},{17,... | collective-permute-start | bytes 786440 | tf_op jit(solution)/shard_map/ppermute | solution.py:15
  77.9 31.2 %collective-permute-start.4 = (bf16[256,512]{0,1:T(8,128)(2,1)}, bf16[256,512]{0,1:T(8,128)(2,1)}, u32[]{:S(2)}, u32[]{:S(2)}) collective-permute-start(bf16[256,512]{0,1:T(8,128)(2,1)} %bitcast.19), channel_id=1, source_target_pairs={{0,2},{1,3},{2,4},{3,5},{4,6},{5,7},{8,10},{9,11},{10,12},{11,13},... | collective-permute-start | bytes 786440 | tf_op jit(solution)/shard_map/ppermute | solution.py:15
  84.7 27.3 %collective-permute-start.3 = (bf16[256,512]{0,1:T(8,128)(2,1)}, bf16[256,512]{0,1:T(8,128)(2,1)}, u32[]{:S(2)}, u32[]{:S(2)}) collective-permute-start(bf16[256,512]{0,1:T(8,128)(2,1)} %bitcast.19), channel_id=1, source_target_pairs={{0,1},{1,2},{2,3},{3,4},{4,5},{5,6},{6,7},{8,9},{9,10},{10,11},{11... | collective-permute-start | bytes 786440 | tf_op jit(solution)/shard_map/ppermute | solution.py:15
  88.9 25.2 %collective-permute-start.2 = (bf16[256,512]{1,0:T(8,128)(2,1)}, bf16[256,512]{1,0:T(8,128)(2,1)}, u32[]{:S(2)}, u32[]{:S(2)}) collective-permute-start(bf16[256,512]{1,0:T(8,128)(2,1)} %bitcast.398), channel_id=1, source_target_pairs={{0,4},{1,5},{2,6},{3,7},{8,12},{9,13},{10,14},{11,15},{16,20},{17,... | collective-permute-start | bytes 786440 | tf_op jit(solution)/shard_map/ppermute | solution.py:15
  90.8 8.0 %copy-start.31 = (s32[1,3,8]{2,0,1:T(1,128)S(1)}, s32[1,3,8]{2,0,1:T(1,128)}, u32[]{:S(2)}) copy-start(s32[1,3,8]{2,0,1:T(1,128)} %param.9) | copy-start | bytes 292
  90.8 10.6 %copy-start.28 = (bf16[1,256,512]{2,1,0:T(8,128)(2,1)S(1)}, bf16[1,256,512]{2,1,0:T(8,128)(2,1)}, u32[]{:S(2)}) copy-start(bf16[1,256,512]{2,1,0:T(8,128)(2,1)} %param.8) | copy-start | bytes 786436
  96.0 10.1 %copy-start.29 = (bf16[1,256,512]{2,1,0:T(8,128)(2,1)S(1)}, bf16[1,256,512]{2,1,0:T(8,128)(2,1)}, u32[]{:S(2)}) copy-start(bf16[1,256,512]{2,1,0:T(8,128)(2,1)} %param.8) | copy-start | bytes 786436
  96.0 92.4 %collective-permute-start.10 = (bf16[1024,2048]{1,0:T(8,128)(2,1)}, bf16[1024,2048]{1,0:T(8,128)(2,1)}, u32[]{:S(2)}, u32[]{:S(2)}) collective-permute-start(bf16[1024,2048]{1,0:T(8,128)(2,1)} %maximum_select_fusion.1), channel_id=1, source_target_pairs={{0,16},{1,17},{2,18},{3,19},{4,20},{5,21},{6,22},{7,23},{8,24},{9,... | collective-permute-start | bytes 12582920 | tf_op jit(solution)/shard_map/ppermute | solution.py:55
  106.2 9.5 %collective-permute-start.1 = (bf16[256,512]{1,0:T(8,128)(2,1)S(1)}, bf16[256,512]{1,0:T(8,128)(2,1)}, u32[]{:S(2)}, u32[]{:S(2)}) collective-permute-start(bf16[256,512]{1,0:T(8,128)(2,1)S(1)} %bitcast.399), channel_id=1, source_target_pairs={{0,2},{1,3},{2,4},{3,5},{4,6},{5,7},{8,10},{9,11},{10,12},{11,13},... | collective-permute-start | bytes 786440 | tf_op jit(solution)/shard_map/ppermute | solution.py:15
  109.1 8.3 %collective-permute-start = (bf16[256,512]{1,0:T(8,128)(2,1)S(1)}, bf16[256,512]{1,0:T(8,128)(2,1)}, u32[]{:S(2)}, u32[]{:S(2)}) collective-permute-start(bf16[256,512]{1,0:T(8,128)(2,1)S(1)} %bitcast.400), channel_id=1, source_target_pairs={{0,1},{1,2},{2,3},{3,4},{4,5},{5,6},{6,7},{8,9},{9,10},{10,11},{11... | collective-permute-start | bytes 786440 | tf_op jit(solution)/shard_map/ppermute | solution.py:15
  120.0 10.7 %copy-start.14 = (bf16[640,4,128]{2,0,1:T(8,128)(2,1)}, bf16[640,4,128]{2,0,1:T(8,128)(2,1)S(1)}, u32[]{:S(2)}) copy-start(bf16[640,4,128]{2,0,1:T(8,128)(2,1)S(1)} %pad_maximum_fusion.5) | copy-start | bytes 1966084
  122.2 3.5 %copy-start.30 = (pred[256,640]{0,1:T(8,128)(4,1)S(1)}, pred[256,640]{0,1:T(8,128)(4,1)}, u32[]{:S(2)}) copy-start(pred[256,640]{0,1:T(8,128)(4,1)} %fusion.50) | copy-start | bytes 491524
  133.2 2.5 copy-start.13
  135.3 2.1 copy-start.12
  137.1 2.3 copy-start.11
  197.9 7.9 %copy-start.7 = (bf16[2048,256]{1,0:T(8,128)(2,1)S(1)}, bf16[2048,256]{1,0:T(8,128)(2,1)}, u32[]{:S(2)}) copy-start(bf16[2048,256]{1,0:T(8,128)(2,1)} %copy-done.6) | copy-start | bytes 3145732
  249.6 2.7 copy-start.8
  249.6 2.7 copy-start.9
  249.6 2.7 copy-start.10
  253.5 1.6 copy-start.2
  253.5 2.1 copy-start.3
  254.4 1.8 copy-start.4
  256.2 6.7 %copy-start.15 = (bf16[128,4,256]{2,0,1:T(8,128)(2,1)S(1)}, bf16[128,4,256]{2,0,1:T(8,128)(2,1)}, u32[]{:S(2)}) copy-start(bf16[128,4,256]{2,0,1:T(8,128)(2,1)} %get-tuple-element.37) | copy-start | bytes 786436
  256.2 6.7 %copy-start.16 = (bf16[128,4,256]{2,0,1:T(8,128)(2,1)S(1)}, bf16[128,4,256]{2,0,1:T(8,128)(2,1)}, u32[]{:S(2)}) copy-start(bf16[128,4,256]{2,0,1:T(8,128)(2,1)} %get-tuple-element.39) | copy-start | bytes 786436
  256.2 6.7 %copy-start.17 = (bf16[128,4,256]{2,0,1:T(8,128)(2,1)S(1)}, bf16[128,4,256]{2,0,1:T(8,128)(2,1)}, u32[]{:S(2)}) copy-start(bf16[128,4,256]{2,0,1:T(8,128)(2,1)} %get-tuple-element.41) | copy-start | bytes 786436
  256.2 6.7 %copy-start.18 = (bf16[128,4,256]{2,0,1:T(8,128)(2,1)S(1)}, bf16[128,4,256]{2,0,1:T(8,128)(2,1)}, u32[]{:S(2)}) copy-start(bf16[128,4,256]{2,0,1:T(8,128)(2,1)} %get-tuple-element.43) | copy-start | bytes 786436
  258.5 20.9 %collective-permute-start.11 = (f32[128,512]{1,0:T(8,128)}, f32[128,512]{1,0:T(8,128)}, u32[]{:S(2)}, u32[]{:S(2)}) collective-permute-start(f32[128,512]{1,0:T(8,128)} %copy.105), channel_id=1, source_target_pairs={{1,0},{2,1},{3,2},{4,3},{5,4},{6,5},{7,6},{9,8},{10,9},{11,10},{12... | collective-permute-start | bytes 786440 | tf_op jit(solution)/shard_map/ppermute | solution.py:15
  261.6 20.3 %collective-permute-start.14 = (f32[128,512]{1,0:T(8,128)}, f32[128,512]{1,0:T(8,128)}, u32[]{:S(2)}, u32[]{:S(2)}) collective-permute-start(f32[128,512]{1,0:T(8,128)} %copy.118), channel_id=1, source_target_pairs={{1,0},{2,1},{3,2},{4,3},{5,4},{6,5},{7,6},{9,8},{10,9},{11,10},{12... | collective-permute-start | bytes 786440 | tf_op jit(solution)/shard_map/ppermute | solution.py:15
  271.3 1.4 copy-start.25
  271.3 1.6 copy-start.26
  272.9 1.6 slice-start
  273.1 1.7 copy-start.20
  273.1 3.1 copy-start.19
  274.5 3.1 slice-start.1
  274.5 3.3 %copy-start.22 = (f32[128,4,128]{0,2,1:T(8,128)S(1)}, f32[128,4,128]{0,2,1:T(8,128)}, u32[]{:S(2)}) copy-start(f32[128,4,128]{0,2,1:T(8,128)} %get-tuple-element.13) | copy-start | bytes 786436
  274.5 4.8 %copy-start.21 = (f32[128,4,128]{0,2,1:T(8,128)S(1)}, f32[128,4,128]{0,2,1:T(8,128)}, u32[]{:S(2)}) copy-start(f32[128,4,128]{0,2,1:T(8,128)} %get-tuple-element.12) | copy-start | bytes 786436
  274.9 14.0 %collective-permute-start.12 = (f32[128,512]{1,0:T(8,128)S(1)}, f32[128,512]{1,0:T(8,128)}, u32[]{:S(2)}, u32[]{:S(2)}) collective-permute-start(f32[128,512]{1,0:T(8,128)S(1)} %copy.107), channel_id=1, source_target_pairs={{2,0},{3,1},{4,2},{5,3},{6,4},{7,5},{10,8},{11,9},{12,10},{13,11},... | collective-permute-start | bytes 786440 | tf_op jit(solution)/shard_map/ppermute | solution.py:15
  276.3 30.7 %collective-permute-start.13 = (f32[128,512]{1,0:T(8,128)S(1)}, f32[128,512]{1,0:T(8,128)S(1)}, u32[]{:S(2)}, u32[]{:S(2)}) collective-permute-start(f32[128,512]{1,0:T(8,128)S(1)} %copy.108), channel_id=1, source_target_pairs={{4,0},{5,1},{6,2},{7,3},{12,8},{13,9},{14,10},{15,11},{20,16},{21,... | collective-permute-start | bytes 786440 | tf_op jit(solution)/shard_map/ppermute | solution.py:15
  278.0 15.6 %collective-permute-start.15 = (f32[128,512]{1,0:T(8,128)S(1)}, f32[128,512]{1,0:T(8,128)}, u32[]{:S(2)}, u32[]{:S(2)}) collective-permute-start(f32[128,512]{1,0:T(8,128)S(1)} %copy.120), channel_id=1, source_target_pairs={{2,0},{3,1},{4,2},{5,3},{6,4},{7,5},{10,8},{11,9},{12,10},{13,11},... | collective-permute-start | bytes 786440 | tf_op jit(solution)/shard_map/ppermute | solution.py:15
  279.4 36.0 %collective-permute-start.16 = (f32[128,512]{1,0:T(8,128)S(1)}, f32[128,512]{1,0:T(8,128)S(1)}, u32[]{:S(2)}, u32[]{:S(2)}) collective-permute-start(f32[128,512]{1,0:T(8,128)S(1)} %copy.121), channel_id=1, source_target_pairs={{4,0},{5,1},{6,2},{7,3},{12,8},{13,9},{14,10},{15,11},{20,16},{21,... | collective-permute-start | bytes 786440 | tf_op jit(solution)/shard_map/ppermute | solution.py:15
  280.7 35.5 %copy-start.1 = (bf16[1,256,2048]{2,1,0:T(8,128)(2,1)S(1)}, bf16[1,256,2048]{2,1,0:T(8,128)(2,1)}, u32[]{:S(2)}) copy-start(bf16[1,256,2048]{2,1,0:T(8,128)(2,1)} %param.11) | copy-start | bytes 3145732
  (3 other events, 3.4 us)
